TPU v7x, 128 devices: a whole 4x4x4 slice. The times are simulated.
128 devices in a mesh: dp: 4 (over y_lo, core), pipe: 4 (over z), seq: 8 (over y_hi, x).
Axes of the slice: x: 4, y: 4 (y_hi: 2, y_lo: 2; y = y_hi * 2 + y_lo), z: 4, core: 2. Of those that a mesh axis runs over, the one named last changes fastest.
Arguments:
- layer_input: bfloat16 [4, 4, 2048, 4096], P('dp', 'pipe', 'seq'), may hold values from -0.09375 to 0.09375
- queries: bfloat16 [4, 4, 2048, 4096], P('dp', 'pipe', 'seq'), may hold values from -6 to 6
- keys: bfloat16 [4, 4, 2048, 512], P('dp', 'pipe', 'seq'), may hold values from -6 to 6
- values: bfloat16 [4, 4, 2048, 512], P('dp', 'pipe', 'seq'), may hold values from -6 to 6
- attn_out: bfloat16 [4, 4, 2048, 4096], P('dp', 'pipe', 'seq'), may hold values from -6 to 6
- out_grad: bfloat16 [4, 4, 2048, 4096], P('dp', 'pipe', 'seq'), may hold values from -6 to 6
- log_norm: bfloat16 [4, 4, 2048, 32], P('dp', 'pipe', 'seq'), may hold values from 2 to 6
- segment_ids: int32 [4, 4, 2048], P('dp', 'pipe'), may hold values from 0 to 7, never falling along the last dimension, each value on 1 to 1024 neighbouring positions
- key_weight: bfloat16 [4, 4096, 512], P('pipe'), may hold values from -0.25 to 0.25
- value_weight: bfloat16 [4, 4096, 512], P('pipe'), may hold values from -0.25 to 0.25
Outputs:
- query_grad: bfloat16 [4, 4, 2048, 4096], P('dp', 'pipe', 'seq')
- upstream_grad: bfloat16 [4, 4, 2048, 4096], P('dp', 'pipe', 'seq')
- key_weight_grad: float32 [4, 4096, 512], P('pipe', ('dp', 'seq'))
- value_weight_grad: float32 [4, 4096, 512], P('pipe', ('dp', 'seq'))
Inputs may be any that keep to these rules, and one draw needn't show every extreme that they name: `segment_ids`: along each sequence the document ids never fall; each document holds 1 to 1024 tokens, and one holds exactly 1024.
All inputs are finite; a program needn't handle non-finite values.
Results may differ from a plain program's by a relative error of at most 0.0063.
Values may be sent and summed in bfloat16 or wider, within the bound.
A program may use at most 128 MiB of HBM per device.

v0:
```python
import math

import jax
import jax.numpy as jnp
from jax import lax
from jax.sharding import PartitionSpec as P

HQ = 32
KVH = 4
HD = 128


def shifted(value, axis, steps):
    count = lax.axis_size(axis)
    initial, last = (max(0, -steps), min(count, count - steps))
    return lax.ppermute(value, axis, [(source, source + steps) for source in range(initial, last)])


def attend(
    query_block,
    grad_block,
    norm_block,
    delta_block,
    row_seg,
    row_pos,
    head_keys,
    head_values,
    col_seg,
    col_pos,
):
    score_scale = 1.0 / math.sqrt(HD)
    scores = (
        lax.dot_general(
            query_block, head_keys, (((1,), (1,)), ((), ())), preferred_element_type=jnp.float32
        )
        * score_scale
    )
    allowed = (row_seg[:, None] == col_seg[None, :]) & (col_pos[None, :] <= row_pos[:, None])
    probability = jnp.exp(
        jnp.where(allowed, scores - norm_block.astype(jnp.float32)[:, None], -1e30)
    )
    grad_v = lax.dot_general(
        probability.astype(jnp.bfloat16),
        grad_block,
        (((0,), (0,)), ((), ())),
        preferred_element_type=jnp.float32,
    )
    grad_prob = lax.dot_general(
        grad_block, head_values, (((1,), (1,)), ((), ())), preferred_element_type=jnp.float32
    )
    grad_score = (probability * (grad_prob - delta_block.astype(jnp.float32)[:, None])).astype(
        jnp.bfloat16
    )
    grad_q = jnp.dot(grad_score, head_keys, preferred_element_type=jnp.float32) * score_scale
    grad_k = (
        lax.dot_general(
            grad_score, query_block, (((0,), (0,)), ((), ())), preferred_element_type=jnp.float32
        )
        * score_scale
    )
    return (grad_q, grad_k, grad_v)


def row_delta(grad_rows, out_rows, heads):
    product = grad_rows.astype(jnp.float32) * out_rows.astype(jnp.float32)
    return jnp.sum(product.reshape(product.shape[0], heads, HD), axis=-1).astype(jnp.bfloat16)


def shards(
    layer_input,
    queries,
    keys,
    values,
    attn_out,
    out_grad,
    log_norm,
    segment_ids,
    key_weight,
    value_weight,
):
    inputs = layer_input[0, 0]
    query_rows = queries[0, 0]
    key_rows = keys[0, 0]
    value_rows = values[0, 0]
    out_rows = attn_out[0, 0]
    grad_rows = out_grad[0, 0]
    norm_rows = log_norm[0, 0]
    segments = segment_ids[0, 0]
    weight_k = key_weight[0]
    weight_v = value_weight[0]
    tokens = query_rows.shape[0]
    seq_devices = lax.axis_size("seq")
    seq_len = tokens * seq_devices
    group_size = HQ // KVH
    positions = jnp.arange(seq_len, dtype=jnp.int32)
    key_all, value_all = (
        lax.all_gather(key_rows, "seq", axis=0, tiled=True),
        lax.all_gather(value_rows, "seq", axis=0, tiled=True),
    )
    local_delta = row_delta(grad_rows, out_rows, HQ)
    returned = False
    local_heads = HQ // seq_devices
    head_q, head_grad, head_norm, head_delta = (
        lax.all_to_all(query_rows, "seq", split_axis=1, concat_axis=0, tiled=True),
        lax.all_to_all(grad_rows, "seq", split_axis=1, concat_axis=0, tiled=True),
        lax.all_to_all(norm_rows, "seq", split_axis=1, concat_axis=0, tiled=True),
        lax.all_to_all(local_delta, "seq", split_axis=1, concat_axis=0, tiled=True),
    )
    first_head = lax.axis_index("seq") * local_heads
    block_rows = math.gcd(seq_len, 512)
    blocks = seq_len // block_rows

    def one_head(head_index):
        kv_index = (first_head + head_index) // group_size
        head_keys = lax.dynamic_slice_in_dim(key_all, kv_index * HD, HD, 1)
        head_values = lax.dynamic_slice_in_dim(value_all, kv_index * HD, HD, 1)
        col_q = lax.dynamic_slice_in_dim(head_q, head_index * HD, HD, 1)
        col_grad = lax.dynamic_slice_in_dim(head_grad, head_index * HD, HD, 1)
        col_norm = lax.dynamic_index_in_dim(head_norm, head_index, 1, keepdims=False)
        col_delta = lax.dynamic_index_in_dim(head_delta, head_index, 1, keepdims=False)

        def block_step(totals, number):
            row_begin = number * block_rows
            grad_q, grad_k, grad_v = attend(
                lax.dynamic_slice_in_dim(col_q, row_begin, block_rows, 0),
                lax.dynamic_slice_in_dim(col_grad, row_begin, block_rows, 0),
                lax.dynamic_slice_in_dim(col_norm, row_begin, block_rows, 0),
                lax.dynamic_slice_in_dim(col_delta, row_begin, block_rows, 0),
                lax.dynamic_slice_in_dim(segments, row_begin, block_rows, 0),
                lax.dynamic_slice_in_dim(positions, row_begin, block_rows, 0),
                head_keys,
                head_values,
                segments,
                positions,
            )
            return ((totals[0] + grad_k, totals[1] + grad_v), grad_q)

        empty_rows = jnp.zeros((seq_len, HD), jnp.float32)
        (key_total, value_total), pieces = lax.scan(
            block_step, (empty_rows, empty_rows), jnp.arange(blocks, dtype=jnp.int32)
        )
        return (pieces.reshape(seq_len, HD), key_total, value_total, kv_index)

    stacked_q, stacked_k, stacked_v, kv_owner = lax.map(
        one_head, jnp.arange(local_heads, dtype=jnp.int32)
    )
    head_dq = stacked_q.transpose(1, 0, 2).reshape(seq_len, local_heads * HD).astype(jnp.bfloat16)
    query_grad = lax.all_to_all(head_dq, "seq", split_axis=0, concat_axis=1, tiled=True)
    owner_table = (kv_owner[:, None] == jnp.arange(KVH, dtype=jnp.int32)[None, :]).astype(
        jnp.float32
    )
    part_k = jnp.einsum(
        "hk,hld->lkd", owner_table, stacked_k, precision=lax.Precision.HIGHEST
    ).reshape(seq_len, KVH * HD)
    part_v = jnp.einsum(
        "hk,hld->lkd", owner_table, stacked_v, precision=lax.Precision.HIGHEST
    ).reshape(seq_len, KVH * HD)
    key_total, value_total = (
        lax.psum_scatter(part_k, "seq", scatter_dimension=0, tiled=True),
        lax.psum_scatter(part_v, "seq", scatter_dimension=0, tiled=True),
    )
    key_grad = key_total.astype(jnp.bfloat16)
    value_grad = value_total.astype(jnp.bfloat16)
    local_wk = lax.dot_general(
        inputs, key_grad, (((0,), (0,)), ((), ())), preferred_element_type=jnp.float32
    )
    local_wv = lax.dot_general(
        inputs, value_grad, (((0,), (0,)), ((), ())), preferred_element_type=jnp.float32
    )
    grad_wk, grad_wv = (
        lax.psum_scatter(local_wk, ("dp", "seq"), scatter_dimension=0, tiled=True),
        lax.psum_scatter(local_wv, ("dp", "seq"), scatter_dimension=0, tiled=True),
    )
    input_grad = lax.dot_general(
        key_grad, weight_k, (((1,), (1,)), ((), ())), preferred_element_type=jnp.float32
    )
    input_grad = input_grad + lax.dot_general(
        value_grad, weight_v, (((1,), (1,)), ((), ())), preferred_element_type=jnp.float32
    )
    upstream = shifted(input_grad.astype(jnp.bfloat16), "pipe", -1)
    return (query_grad[None, None], upstream[None, None], grad_wk[None], grad_wv[None])


def solution(mesh):
    return jax.shard_map(
        shards,
        mesh=mesh,
        in_specs=(
            P("dp", "pipe", "seq", None),
            P("dp", "pipe", "seq", None),
            P("dp", "pipe", "seq", None),
            P("dp", "pipe", "seq", None),
            P("dp", "pipe", "seq", None),
            P("dp", "pipe", "seq", None),
            P("dp", "pipe", "seq", None),
            P("dp", "pipe", None),
            P("pipe", None, None),
            P("pipe", None, None),
        ),
        out_specs=(
            P("dp", "pipe", "seq", None),
            P("dp", "pipe", "seq", None),
            P("pipe", ("dp", "seq"), None),
            P("pipe", ("dp", "seq"), None),
        ),
        check_vma=False,
    )
```

profile of v0, /device:TPU:0, one launch (start us, length us, event | category | flops | bytes accessed | tf_op | source)
XLA Modules:
  0.0 1121.0 jit_solution(11875083008240548673)
XLA Ops:
  9.2 7.0 all-to-all-start.2
  16.3 2.9 multiply_bitcast_fusion
  19.2 2.7 copy.66
  21.9 3.5 reduce_sum.9
  26.1 7.2 all-to-all-start.3
  37.8 3.2 all-to-all-done.3
  41.0 4.3 all-to-all-start
  50.6 27.1 %all-to-all-done = bf16[256,8,512]{2,0,1:T(8,128)(2,1)} async-done(((bf16[256,8,512]{2,0,1:T(8,128)(2,1)}), bf16[256,8,512]{2,0,1:T(8,128)(2,1)}, u32[]{:S(2)}, u32[]{:S(2)}) %all-to-all-start) | async-done | bytes 2097184 | tf_op jit(solution)/shard_map/all_to_all | solution.py:104
  77.8 6.4 all-to-all-start.1
  84.5 27.6 %all-to-all-done.1 = bf16[256,8,512]{2,0,1:T(8,128)(2,1)} async-done(((bf16[256,8,512]{2,0,1:T(8,128)(2,1)}), bf16[256,8,512]{2,0,1:T(8,128)(2,1)}, u32[]{:S(2)}, u32[]{:S(2)}) %all-to-all-start.1) | async-done | bytes 2097184 | tf_op jit(solution)/shard_map/all_to_all | solution.py:105
  112.1 45.2 %all-gather.7.cloned.1.call-done = bf16[1,1,2048,512]{3,2,1,0:T(8,128)(2,1)} async-done(((bf16[1,1,256,512]{3,2,1,0:T(8,128)(2,1)}), bf16[1,1,2048,512]{3,2,1,0:T(8,128)(2,1)}) %all-gather.7.cloned.1.call-update) | async-done | bytes 2097168 | tf_op jit(solution)/shard_map/all_gather | solution.py:98
  157.3 424.7 %while.54 = (s32[]{:T(128)}, bf16[4,2048,128]{2,1,0:T(8,128)(2,1)}, f32[4,2048,128]{2,0,1:T(4,128)}, f32[4,2048,128]{2,0,1:T(4,128)}, s32[4]{0:T(128)S(1)}, /*in...) while((s32[]{:T(128)}, bf16[4,2048,128]{2,1,0:T(8,128)(2,1)}, ...), condition=%wide.region_4.5_spmd.clone.clone, body=%wide.region_1.4_spmd.clone.clone.sunk | while | flops 1354040320 | bytes 53804240 | solution.py:144
  165.9 40.5 %while.55 = (s32[]{:T(128)}, f32[2048,128]{1,0:T(8,128)S(1)}, f32[2048,128]{1,0:T(8,128)}, bf16[4,512,128]{2,1,0:T(8,128)(2,1)}, s32[4]{0:T(128)S(1)}, /*index=5...) while((s32[]{:T(128)}, f32[2048,128]{1,0:T(8,128)S(1)}, ...), condition=%wide.region_3.3_spmd.clone.clone, body=%wide.region_2.2_spmd.clone.clone.sunk | while | flops 1354040320 | bytes 44341716 | solution.py:139
  177.7 2.6 select_exponential_fusion.2
  187.8 2.6 select_exponential_fusion.2
  197.9 2.6 select_exponential_fusion.2
  208.3 27.5 %dynamic_update_slice.48 = f32[4,2048,128]{2,0,1:T(4,128)} dynamic-update-slice(f32[4,2048,128]{2,0,1:T(4,128)} %get-tuple-element.850, f32[1,2048,128]{2,0,1:T(1,128)S(1)} %bitcast.127, s32[]{:T(128)S(6)} %copy.96, s32[]{:T(128)} %constant.97.clone.1..sunk, s32[]{:T(128)} %constant.97.clone.1..sunk) | dynamic-update-slice | bytes 2097156 | tf_op jit(solution)/shard_map/while/body/jit(dynamic_update_index_in_dim)/dynamic_update_slice | solution.py:144
  235.9 27.6 %dynamic_update_slice.49 = f32[4,2048,128]{2,0,1:T(4,128)} dynamic-update-slice(f32[4,2048,128]{2,0,1:T(4,128)} %get-tuple-element.851, f32[1,2048,128]{2,0,1:T(1,128)} %bitcast.128, s32[]{:T(128)S(6)} %copy.96, s32[]{:T(128)} %constant.97.clone.1..sunk, s32[]{:T(128)} %constant.97.clone.1..sunk) | dynamic-update-slice | bytes 2097156 | tf_op jit(solution)/shard_map/while/body/jit(dynamic_update_index_in_dim)/dynamic_update_slice | solution.py:144
  272.1 40.5 %while.55 = (s32[]{:T(128)}, f32[2048,128]{1,0:T(8,128)S(1)}, f32[2048,128]{1,0:T(8,128)}, bf16[4,512,128]{2,1,0:T(8,128)(2,1)}, s32[4]{0:T(128)S(1)}, /*index=5...) while((s32[]{:T(128)}, f32[2048,128]{1,0:T(8,128)S(1)}, ...), condition=%wide.region_3.3_spmd.clone.clone, body=%wide.region_2.2_spmd.clone.clone.sunk | while | flops 1354040320 | bytes 44341716 | solution.py:139
  273.7 2.6 select_exponential_fusion.2
  283.8 2.6 select_exponential_fusion.2
  294.0 2.6 select_exponential_fusion.2
  304.1 2.6 select_exponential_fusion.2
  314.5 27.5 %dynamic_update_slice.48 = f32[4,2048,128]{2,0,1:T(4,128)} dynamic-update-slice(f32[4,2048,128]{2,0,1:T(4,128)} %get-tuple-element.850, f32[1,2048,128]{2,0,1:T(1,128)S(1)} %bitcast.127, s32[]{:T(128)S(6)} %copy.96, s32[]{:T(128)} %constant.97.clone.1..sunk, s32[]{:T(128)} %constant.97.clone.1..sunk) | dynamic-update-slice | bytes 2097156 | tf_op jit(solution)/shard_map/while/body/jit(dynamic_update_index_in_dim)/dynamic_update_slice | solution.py:144
  342.0 27.6 %dynamic_update_slice.49 = f32[4,2048,128]{2,0,1:T(4,128)} dynamic-update-slice(f32[4,2048,128]{2,0,1:T(4,128)} %get-tuple-element.851, f32[1,2048,128]{2,0,1:T(1,128)} %bitcast.128, s32[]{:T(128)S(6)} %copy.96, s32[]{:T(128)} %constant.97.clone.1..sunk, s32[]{:T(128)} %constant.97.clone.1..sunk) | dynamic-update-slice | bytes 2097156 | tf_op jit(solution)/shard_map/while/body/jit(dynamic_update_index_in_dim)/dynamic_update_slice | solution.py:144
  378.3 40.5 %while.55 = (s32[]{:T(128)}, f32[2048,128]{1,0:T(8,128)S(1)}, f32[2048,128]{1,0:T(8,128)}, bf16[4,512,128]{2,1,0:T(8,128)(2,1)}, s32[4]{0:T(128)S(1)}, /*index=5...) while((s32[]{:T(128)}, f32[2048,128]{1,0:T(8,128)S(1)}, ...), condition=%wide.region_3.3_spmd.clone.clone, body=%wide.region_2.2_spmd.clone.clone.sunk | while | flops 1354040320 | bytes 44341716 | solution.py:139
  379.9 2.6 select_exponential_fusion.2
  390.0 2.6 select_exponential_fusion.2
  400.2 2.6 select_exponential_fusion.2
  420.7 27.5 %dynamic_update_slice.48 = f32[4,2048,128]{2,0,1:T(4,128)} dynamic-update-slice(f32[4,2048,128]{2,0,1:T(4,128)} %get-tuple-element.850, f32[1,2048,128]{2,0,1:T(1,128)S(1)} %bitcast.127, s32[]{:T(128)S(6)} %copy.96, s32[]{:T(128)} %constant.97.clone.1..sunk, s32[]{:T(128)} %constant.97.clone.1..sunk) | dynamic-update-slice | bytes 2097156 | tf_op jit(solution)/shard_map/while/body/jit(dynamic_update_index_in_dim)/dynamic_update_slice | solution.py:144
  448.2 27.6 %dynamic_update_slice.49 = f32[4,2048,128]{2,0,1:T(4,128)} dynamic-update-slice(f32[4,2048,128]{2,0,1:T(4,128)} %get-tuple-element.851, f32[1,2048,128]{2,0,1:T(1,128)} %bitcast.128, s32[]{:T(128)S(6)} %copy.96, s32[]{:T(128)} %constant.97.clone.1..sunk, s32[]{:T(128)} %constant.97.clone.1..sunk) | dynamic-update-slice | bytes 2097156 | tf_op jit(solution)/shard_map/while/body/jit(dynamic_update_index_in_dim)/dynamic_update_slice | solution.py:144
  484.5 40.5 %while.55 = (s32[]{:T(128)}, f32[2048,128]{1,0:T(8,128)S(1)}, f32[2048,128]{1,0:T(8,128)}, bf16[4,512,128]{2,1,0:T(8,128)(2,1)}, s32[4]{0:T(128)S(1)}, /*index=5...) while((s32[]{:T(128)}, f32[2048,128]{1,0:T(8,128)S(1)}, ...), condition=%wide.region_3.3_spmd.clone.clone, body=%wide.region_2.2_spmd.clone.clone.sunk | while | flops 1354040320 | bytes 44341716 | solution.py:139
  486.1 2.6 select_exponential_fusion.2
  526.9 27.5 %dynamic_update_slice.48 = f32[4,2048,128]{2,0,1:T(4,128)} dynamic-update-slice(f32[4,2048,128]{2,0,1:T(4,128)} %get-tuple-element.850, f32[1,2048,128]{2,0,1:T(1,128)S(1)} %bitcast.127, s32[]{:T(128)S(6)} %copy.96, s32[]{:T(128)} %constant.97.clone.1..sunk, s32[]{:T(128)} %constant.97.clone.1..sunk) | dynamic-update-slice | bytes 2097156 | tf_op jit(solution)/shard_map/while/body/jit(dynamic_update_index_in_dim)/dynamic_update_slice | solution.py:144
  554.4 27.6 %dynamic_update_slice.49 = f32[4,2048,128]{2,0,1:T(4,128)} dynamic-update-slice(f32[4,2048,128]{2,0,1:T(4,128)} %get-tuple-element.851, f32[1,2048,128]{2,0,1:T(1,128)} %bitcast.128, s32[]{:T(128)S(6)} %copy.96, s32[]{:T(128)} %constant.97.clone.1..sunk, s32[]{:T(128)} %constant.97.clone.1..sunk) | dynamic-update-slice | bytes 2097156 | tf_op jit(solution)/shard_map/while/body/jit(dynamic_update_index_in_dim)/dynamic_update_slice | solution.py:144
  582.0 6.5 fusion.25
  591.2 6.5 fusion.27
  600.2 74.6 %reduce-scatter.7.cloned.1.call-done = f32[256,512]{1,0:T(8,128)} async-done(((f32[2048,512]{1,0:T(8,128)}), f32[256,512]{1,0:T(8,128)}) %reduce-scatter.7.cloned.1.call-update) | async-done | bytes 524304 | tf_op jit(solution)/shard_map/reduce_scatter | solution.py:160
  674.8 5.6 convolution_bitcast_fusion
  680.5 81.8 %reduce-scatter.5.cloned.1.call-done = f32[256,512]{1,0:T(8,128)} async-done(((f32[2048,512]{1,0:T(8,128)}), f32[256,512]{1,0:T(8,128)}) %reduce-scatter.5.cloned.1.call-update) | async-done | bytes 524304 | tf_op jit(solution)/shard_map/reduce_scatter | solution.py:159
  762.3 5.5 convolution_bitcast_fusion.1
  768.9 3.6 fusion.16
  776.5 4.0 copy.52
  783.2 44.4 %all_to_all.86 = bf16[8,256,512]{1,2,0:T(8,128)(2,1)} all-to-all(bf16[8,256,512]{1,2,0:T(8,128)(2,1)S(1)} %copy.53), channel_id=1, replica_groups=mesh['dp'=4,'pipe'=4,'seq'=8] {'seq'}, dimensions={0} | all-to-all | bytes 4194304 | tf_op jit(solution)/shard_map/all_to_all | solution.py:148
  827.6 4.1 copy.56
  831.6 109.0 %reduce-scatter.11.cloned.1.call-done = f32[128,512]{0,1:T(8,128)} async-done(((f32[4096,512]{0,1:T(8,128)}), f32[128,512]{0,1:T(8,128)}) %reduce-scatter.11.cloned.1.call-update) | async-done | bytes 262160 | tf_op jit(solution)/shard_map/reduce_scatter | solution.py:172
  942.4 166.8 %reduce-scatter.9.cloned.1.call-done = f32[128,512]{0,1:T(8,128)} async-done(((f32[4096,512]{0,1:T(8,128)}), f32[128,512]{0,1:T(8,128)}) %reduce-scatter.9.cloned.1.call-update) | async-done | bytes 262160 | tf_op jit(solution)/shard_map/reduce_scatter | solution.py:171
  1111.0 3.1 copy.107
  (446 shorter events, 177.9 us)
Async XLA Ops:
  7.2 667.6 %copy-start = (bf16[1,1,256,4096]{3,2,1,0:T(8,128)(2,1)S(1)}, bf16[1,1,256,4096]{3,2,1,0:T(8,128)(2,1)}, u32[]{:S(2)}) copy-start(bf16[1,1,256,4096]{3,2,1,0:T(8,128)(2,1)} %param.14) | copy-start | bytes 6291460
  7.2 104.9 %all-gather.5.cloned.1.call-start = ((), (), s32[]{:S(2)}) async-start(), calls=%async_computation.13 | async-start | bytes 2359296 | tf_op jit(solution)/shard_map/all_gather | solution.py:97
  9.2 16.9 %all-to-all-start.2 = ((bf16[256,8,4]{0,2,1:T(4,128)(2,1)}), bf16[256,8,4]{0,2,1:T(4,128)(2,1)S(1)}, u32[]{:S(2)}, u32[]{:S(2)}) async-start(bf16[256,8,4]{0,2,1:T(4,128)(2,1)} %all_to_all.72), calls=%async_computation.2 | async-start | bytes 32768 | tf_op jit(solution)/shard_map/all_to_all | solution.py:106
  26.1 14.9 %all-to-all-start.3 = ((bf16[256,8,4]{0,2,1:T(4,128)(2,1)}), bf16[256,8,4]{0,2,1:T(4,128)(2,1)S(1)}, u32[]{:S(2)}, u32[]{:S(2)}) async-start(bf16[256,8,4]{0,2,1:T(4,128)(2,1)} %convert_element_type.60), calls=%async_computation.3 | async-start | bytes 32768 | tf_op jit(solution)/shard_map/all_to_all | solution.py:107
  41.0 36.8 %all-to-all-start = ((bf16[256,8,512]{2,0,1:T(8,128)(2,1)}), bf16[256,8,512]{2,0,1:T(8,128)(2,1)}, u32[]{:S(2)}, u32[]{:S(2)}) async-start(bf16[256,8,512]{2,0,1:T(8,128)(2,1)} %copy.49), calls=%async_computation | async-start | bytes 4194304 | tf_op jit(solution)/shard_map/all_to_all | solution.py:104
  45.4 111.9 %all-gather.7.cloned.1.call-start = ((), (), s32[]{:S(2)}) async-start(), calls=%async_computation.14 | async-start | bytes 2359296 | tf_op jit(solution)/shard_map/all_gather | solution.py:98
  48.6 108.7 %copy-start.11 = (s32[1,1,2048]{2,1,0:T(1,128)S(1)}, s32[1,1,2048]{2,1,0:T(1,128)}, u32[]{:S(2)}) copy-start(s32[1,1,2048]{2,1,0:T(1,128)} %param.21) | copy-start | bytes 24580
  77.8 34.3 %all-to-all-start.1 = ((bf16[256,8,512]{2,0,1:T(8,128)(2,1)}), bf16[256,8,512]{2,0,1:T(8,128)(2,1)}, u32[]{:S(2)}, u32[]{:S(2)}) async-start(bf16[256,8,512]{2,0,1:T(8,128)(2,1)} %copy.50), calls=%async_computation.1 | async-start | bytes 4194304 | tf_op jit(solution)/shard_map/all_to_all | solution.py:105
  84.2 590.6 %reduce-scatter.7.cloned.1.call-start = ((), (), s32[]{:S(2)}) async-start(), calls=%async_computation.10 | async-start | bytes 4718592 | tf_op jit(solution)/shard_map/reduce_scatter | solution.py:160
  167.3 2.9 copy-start.1
  167.3 2.9 copy-start.5
  177.4 2.9 copy-start.1
  177.4 2.9 copy-start.5
  181.5 2.4 copy-start.2
  187.5 2.9 copy-start.1
  187.6 2.9 copy-start.5
  197.7 2.9 copy-start.1
  197.7 2.9 copy-start.5
  273.4 2.9 copy-start.1
  273.5 2.9 copy-start.5
  283.6 2.9 copy-start.1
  283.6 2.9 copy-start.5
  293.7 2.9 copy-start.1
  293.7 2.9 copy-start.5
  303.9 2.9 copy-start.1
  303.9 2.9 copy-start.5
  379.6 2.9 copy-start.1
  379.7 2.9 copy-start.5
  389.8 2.9 copy-start.1
  389.8 2.9 copy-start.5
  399.9 2.9 copy-start.1
  399.9 2.9 copy-start.5
  410.1 2.9 copy-start.1
  410.1 2.9 copy-start.5
  485.8 2.9 copy-start.1
  485.8 2.9 copy-start.5
  496.0 2.9 copy-start.1
  496.0 2.9 copy-start.5
  506.1 2.9 copy-start.1
  506.1 2.9 copy-start.5
  516.3 2.9 copy-start.1
  516.3 2.9 copy-start.5
  590.9 171.3 %reduce-scatter.5.cloned.1.call-start = ((), (), s32[]{:S(2)}) async-start(), calls=%async_computation.9 | async-start | bytes 4718592 | tf_op jit(solution)/shard_map/reduce_scatter | solution.py:159
  600.1 340.5 %reduce-scatter.11.cloned.1.call-start = ((), (), s32[]{:S(2)}) async-start(), calls=%async_computation.12 | async-start | bytes 8650752 | tf_op jit(solution)/shard_map/reduce_scatter | solution.py:172
  680.4 428.8 %reduce-scatter.9.cloned.1.call-start = ((), (), s32[]{:S(2)}) async-start(), calls=%async_computation.11 | async-start | bytes 8650752 | tf_op jit(solution)/shard_map/reduce_scatter | solution.py:171
  768.9 3.6 copy-start.8
  768.9 3.7 copy-start.10
  775.2 56.4 %collective-permute-start = (bf16[256,4096]{1,0:T(8,128)(2,1)}, bf16[256,4096]{1,0:T(8,128)(2,1)}, u32[]{:S(2)}, u32[]{:S(2)}) collective-permute-start(bf16[256,4096]{1,0:T(8,128)(2,1)} %fusion.14), channel_id=1, source_target_pairs={{8,0},{16,8},{24,16},{9,1},{17,9},{25,17},{10,2},{18,10},{26,18},{... | collective-permute-start | bytes 6291464 | tf_op jit(solution)/shard_map/ppermute | solution.py:16
  (80 other events, 139.9 us)
Sparse Core Ops, SparseCore 0:
  10.3 91.4 all-gather.4
  104.1 53.1 all-gather.6
  591.1 83.7 reduce-scatter.6
  678.5 83.6 reduce-scatter.4
  764.5 176.0 reduce-scatter.10
  942.9 166.2 reduce-scatter.8
where the time goes:
time: 1130 us; the launch traced here: 1120 us
  waiting for transfers between devices  537 us (48%)
  local copies, waits for them, and re-layouts  313 us (28%)
  matrix products  151 us (13%)
  blocking collectives  44.4 us (4%)
  starting transfers between devices  26.9 us (2%)
  loops' own time  26.7 us (2%)
  between operations  14.3 us (1%)
    dynamic_update_slice x16, local copies, waits for them, and re-layouts, shards(): lax.map(one_head, jnp.arange(local_heads, dtype=jnp.int32))  229 us
    reduce_scatter x1, waiting for transfers between devices, shards(): lax.psum_scatter(local_wk, ('dp', 'seq'), scatter_dimension=0, tiled=True)  167 us
    reduce_scatter x1, waiting for transfers between devices, shards(): lax.psum_scatter(local_wv, ('dp', 'seq'), scatter_dimension=0, tiled=True)  109 us
    reduce_scatter x1, waiting for transfers between devices, shards(): lax.psum_scatter(part_k, 'seq', scatter_dimension=0, tiled=True)  81.8 us
    reduce_scatter x1, waiting for transfers between devices, shards(): lax.psum_scatter(part_v, 'seq', scatter_dimension=0, tiled=True)  74.6 us
    all_gather x1, waiting for transfers between devices, shards(): lax.all_gather(value_rows, 'seq', axis=0, tiled=True)  45.2 us
    all_to_all x1, blocking collectives, shards(): lax.all_to_all(head_dq, 'seq', split_axis=0, concat_axis=1, tiled=True)  44.4 us
    dot_general x16, matrix products, attend(): lax.dot_general(query_block, head_keys, (((1,), (1,)), ((), ())), preferr...  41.9 us
  transfers between devices with their start and end apart: 11, of which 8 were waited for; matrix products, arithmetic and copies ran while one was open for 5% of the time, Pallas kernels for 0%

commit v1 on v0

v1 whole, which is shorter than its diff:
```python
import functools
import math

import jax
import jax.numpy as jnp
from jax import lax
from jax.experimental import pallas as pl
from jax.experimental.pallas import tpu as pltpu
from jax.sharding import PartitionSpec as P

HQ = 32
KVH = 4
GROUP = HQ // KVH
HD = 128
TOK = 256
HALF = 128
D = 4096
NEAR = 4
SCALE = 1.0 / math.sqrt(HD)
LOG2E = math.log2(math.e)
MASKED = -1e30
MESH = pl.DeviceIdType.MESH
BF = jnp.bfloat16
F32 = jnp.float32


def dot(a, b, ca, cb):
    return lax.dot_general(a, b, (((ca,), (cb,)), ((), ())), preferred_element_type=F32)


def kernel(
    x_hbm, q_hbm, k_hbm, v_hbm, o_hbm, g_hbm, norm_hbm, seg_hbm, wk_hbm, wv_hbm,
    dq_hbm, up_hbm, gk_hbm, gv_hbm,
    q, g, o, norm_in, seg, wk, wv, kv, norm, delta, bias, dqt, dq,
    part_out, part_in, own, grads, pair, xb, up, zeros,
    xs_out, xs_in, ys_out, ys_in, x_own, y_own, x2_out, x2_in, y2_out, y2_in, x_fin, y_fin, gk, gv,
    in_sem, kv_local, xb_local, xb_send, xb_recv, kv_send, kv_recv, part_send, part_recv,
    pair_send, pair_recv, z_send, z_recv, xs_send, xs_recv, ys_send, ys_recv,
    x2_send, x2_recv, y2_send, y2_recv, out_sem,
):
    dp = lax.axis_index("dp")
    p = lax.axis_index("pipe")
    s = lax.axis_index("seq")
    core = lax.rem(dp, 2)
    y_lo = dp // 2
    y_hi = s // 4
    x_at = lax.rem(s, 4)
    y_at = y_hi * 2 + y_lo

    def chip(x, y):
        return (lax.rem(y, 2) * 2 + core, p, (y // 2) * 4 + x)

    def along_x(step):
        return chip(lax.rem(x_at + step, 4), y_at)

    def along_y(step):
        return chip(x_at, lax.rem(y_at + step, 4))

    partner = (y_lo * 2 + 1 - core, p, s)

    def kv_copies():
        for half in range(2):
            for head in range(KVH):
                for which, ref in ((0, k_hbm), (1, v_hbm)):
                    yield pltpu.make_async_copy(
                        ref.at[pl.ds(half * HALF, HALF), pl.ds(head * HD, HD)],
                        kv.at[half, head, which, 0],
                        kv_local.at[half, head, which],
                    )

    copies = list(kv_copies())
    for copy in copies:
        copy.start()
    loads = [
        pltpu.make_async_copy(source, target, in_sem.at[i])
        for i, (source, target) in enumerate(
            ((norm_hbm, norm_in), (seg_hbm, seg), (g_hbm, g), (o_hbm, o), (q_hbm, q), (wk_hbm, wk), (wv_hbm, wv))
        )
    ]
    for copy in loads:
        copy.start()

    def x_columns(block, owner_core):
        y = lax.rem(y_at + block // 4, 4)
        x = lax.rem(x_at + block % 4, 4)
        row = (lax.rem(y, 2) * 2 + owner_core) * 1024 + (y // 2) * 512 + x * 128
        return pl.ds(pl.multiple_of(row, 128), 128)

    def xb_copy(block):
        return pltpu.make_async_copy(
            x_hbm.at[:, x_columns(block, core)], xb.at[0, :, pl.ds(block * 128, 128)], xb_local.at[block]
        )

    def xb_remote(block):
        return pltpu.make_async_remote_copy(
            src_ref=x_hbm.at[:, x_columns(block, 1 - core)],
            dst_ref=xb.at[1, :, pl.ds(block * 128, 128)],
            send_sem=xb_send.at[block],
            recv_sem=xb_recv.at[block],
            device_id=partner,
            device_id_type=MESH,
        )

    def kv_remote(dist, half, head):
        return pltpu.make_async_remote_copy(
            src_ref=kv.at[half, head, :, 0],
            dst_ref=kv.at[half, head, :, dist],
            send_sem=kv_send.at[dist - 1, half, head],
            recv_sem=kv_recv.at[dist - 1, half, head],
            device_id=(dp, p, lax.rem(s + dist, 8)),
            device_id_type=MESH,
        )

    def part_remote(dist, half, head):
        return pltpu.make_async_remote_copy(
            src_ref=part_out.at[half, head, dist - 1],
            dst_ref=part_in.at[half, head, dist - 1],
            send_sem=part_send.at[dist - 1, half, head],
            recv_sem=part_recv.at[dist - 1, half, head],
            device_id=(dp, p, lax.rem(s + 8 - dist, 8)),
            device_id_type=MESH,
        )

    def pair_remote(half, head):
        return pltpu.make_async_remote_copy(
            src_ref=pair.at[head, 0, half],
            dst_ref=pair.at[head, 1, half],
            send_sem=pair_send.at[half, head],
            recv_sem=pair_recv.at[half, head],
            device_id=partner,
            device_id_type=MESH,
        )

    def z_remote(half, chunk):
        return pltpu.make_async_remote_copy(
            src_ref=up.at[pl.ds(half * HALF, HALF), pl.ds(chunk * 1024, 1024)],
            dst_ref=up_hbm.at[pl.ds(half * HALF, HALF), pl.ds(chunk * 1024, 1024)],
            send_sem=z_send.at[half, chunk],
            recv_sem=z_recv.at[half, chunk],
            device_id=(dp, lax.rem(p + 3, 4), s),
            device_id_type=MESH,
        )

    def spread(source, target, send, recv, reach, head, step):
        return pltpu.make_async_remote_copy(
            src_ref=source.at[head, step - 1],
            dst_ref=target.at[head, step - 1],
            send_sem=send.at[head, step - 1],
            recv_sem=recv.at[head, step - 1],
            device_id=reach(step),
            device_id_type=MESH,
        )

    x_first = functools.partial(spread, xs_out, xs_in, xs_send, xs_recv, along_x)
    y_first = functools.partial(spread, ys_out, ys_in, ys_send, ys_recv, along_y)
    x_second = functools.partial(spread, x2_out, x2_in, x2_send, x2_recv, along_y)
    y_second = functools.partial(spread, y2_out, y2_in, y2_send, y2_recv, along_x)

    barrier = pltpu.get_barrier_semaphore()
    peers = [(dp, p, lax.rem(s + i, 8)) for i in range(1, 8)]
    peers += [along_y(i) for i in range(1, 4)]
    peers += [partner, (dp, lax.rem(p + 1, 4), s), (dp, lax.rem(p + 3, 4), s)]
    for peer in peers:
        pl.semaphore_signal(barrier, inc=1, device_id=peer, device_id_type=MESH)
    for copy in copies:
        copy.wait()
    pl.semaphore_wait(barrier, len(peers))

    for half in range(2):
        for head in range(KVH):
            for dist in range(1, NEAR + 1):

                @pl.when(s + dist <= 7)
                def _(dist=dist, half=half, head=head):
                    kv_remote(dist, half, head).start()

                @pl.when(s < dist)
                def _(dist=dist, half=half, head=head):
                    kv[half, head, :, dist] = jnp.zeros((2, HALF, HD), BF)

    for block in range(16):
        xb_copy(block).start()
        xb_remote(block).start()

    loads[0].wait()
    loads[1].wait()
    eye = (
        lax.broadcasted_iota(jnp.int32, (HQ, HQ), 0) == lax.broadcasted_iota(jnp.int32, (HQ, HQ), 1)
    ).astype(F32).astype(BF)
    norm_rows = dot(eye, norm_in[...], 1, 1) * LOG2E
    for head in range(HQ):
        norm[head] = jnp.broadcast_to(norm_rows[head : head + 1], (8, TOK))

    row_seg = seg[:, pl.ds(pl.multiple_of(s * TOK, TOK), TOK)].astype(F32)
    row_seg = jnp.broadcast_to(row_seg, (HALF, TOK))
    row_number = lax.broadcasted_iota(jnp.int32, (HALF, TOK), 1)
    key_number = lax.broadcasted_iota(jnp.int32, (HALF, TOK), 0)

    def document_bias(dist, half):
        block = lax.rem(s + 8 - dist, 8)
        at = pl.multiple_of(block * TOK + half * HALF, HALF)
        key_seg = jnp.broadcast_to(seg[:, pl.ds(at, HALF)].astype(F32), (HALF, HALF)).T
        same = jnp.concatenate([key_seg, key_seg], axis=1) == row_seg
        reach = jnp.where(s >= dist, 0.0, MASKED).astype(F32)
        return jnp.where(same, 0.0, MASKED) + reach

    for half in range(2):
        causal = key_number + half * HALF <= row_number
        bias[half, 0:HALF] = jnp.where(causal, document_bias(0, half), document_bias(NEAR, half))
        for dist in range(1, NEAR):
            bias[half, dist * HALF : (dist + 1) * HALF] = document_bias(dist, half)

    loads[2].wait()
    loads[3].wait()
    ones = jnp.ones((8, HD), BF)

    def delta_head(head, carry):
        at = pl.ds(pl.multiple_of(head * HD, HD), HD)
        product = g[:, at].astype(F32) * o[:, at].astype(F32)
        high = product.astype(BF)
        rest = product - high.astype(F32)
        middle = rest.astype(BF)
        low = (rest - middle.astype(F32)).astype(BF)
        total = dot(ones, high, 1, 1) + dot(ones, middle, 1, 1) + dot(ones, low, 1, 1)
        delta[head] = total.astype(BF).astype(F32)
        return carry

    lax.fori_loop(0, HQ, delta_head, 0, unroll=4)
    loads[4].wait()

    @pl.when(p == 3)
    def _():
        zeros[...] = jnp.zeros((TOK, D), BF)
        fill = pltpu.make_async_copy(zeros, up_hbm, out_sem.at[3])
        fill.start()
        fill.wait()

    def finalize(half, head):
        for dist in range(1, NEAR + 1):

            @pl.when(s + dist <= 7)
            def _(dist=dist):
                part_remote(dist, half, head).wait_recv()
                own[half, head] += part_in[half, head, dist - 1].astype(F32)

        total = own[half, head].astype(BF)
        at = pl.multiple_of(head * HD, HD)
        grads[half, :, pl.ds(at, HD)] = total[0]
        grads[half, :, pl.ds(pl.multiple_of(at + KVH * HD, HD), HD)] = total[1]
        pair[head, 0, half, :, 0:HD] = total[0]
        pair[head, 0, half, :, HD : 2 * HD] = total[1]
        pair_remote(half, head).start()

    def input_grad(half):
        if half == 0:
            loads[5].wait()
            loads[6].wait()
        rows = pl.ds(half * HALF, HALF)

        def chunk_step(chunk, carry):
            for part in range(2):
                at = pl.ds(pl.multiple_of(chunk * 1024 + part * 512, 512), 512)
                total = dot(grads[half, :, 0 : KVH * HD], wk[at, :], 1, 1)
                total = total + dot(grads[half, :, KVH * HD : 2 * KVH * HD], wv[at, :], 1, 1)
                up[rows, at] = total.astype(BF)

            @pl.when(p > 0)
            def _():
                z_remote(half, chunk).start()

            return carry

        lax.fori_loop(0, 4, chunk_step, 0)

    def weight_terms(head):
        pair_remote(0, head).wait_recv()
        pair_remote(1, head).wait_recv()
        both = pair[head].reshape(2 * TOK, 2 * HD)

        def row_of_targets(ry):
            at = pl.ds(ry * 512, 512)
            terms = dot(both, xb[:, :, at].reshape(2 * TOK, 512), 0, 0)
            x_own[head, ry] = terms[0:HD, 0:HD]
            for rx in range(1, 4):
                xs_out[head, rx - 1, ry] = terms[0:HD, rx * HD : (rx + 1) * HD].astype(BF)
            for rx in range(4):
                if ry == 0:
                    y_own[head, rx] = terms[HD : 2 * HD, rx * HD : (rx + 1) * HD]
                else:
                    ys_out[head, ry - 1, rx] = terms[HD : 2 * HD, rx * HD : (rx + 1) * HD].astype(BF)

        for ry in range(4):
            row_of_targets(ry)
        for step in range(1, 4):
            x_first(head, step).start()
            y_first(head, step).start()

    def weight_sums(head):
        for step in range(1, 4):
            x_first(head, step).wait_recv()
            y_first(head, step).wait_recv()
        for r in range(4):
            total = x_own[head, r]
            other = y_own[head, r]
            for step in range(3):
                total = total + xs_in[head, step, r].astype(F32)
                other = other + ys_in[head, step, r].astype(F32)
            if r == 0:
                x_fin[head] = total
                y_fin[head] = other
            else:
                x2_out[head, r - 1] = total.astype(BF)
                y2_out[head, r - 1] = other.astype(BF)
        for step in range(1, 4):
            x_second(head, step).start()
            y_second(head, step).start()

    def weight_final(head):
        for step in range(1, 4):
            x_second(head, step).wait_recv()
            y_second(head, step).wait_recv()
        total = x_fin[head]
        other = y_fin[head]
        for step in range(3):
            total = total + x2_in[head, step].astype(F32)
            other = other + y2_in[head, step].astype(F32)
        at = pl.ds(pl.multiple_of(head * HD, HD), HD)
        gk[:, at] = total.T
        gv[:, at] = other.T

    def attend(half, head, middle):
        for dist in range(1, NEAR + 1):

            @pl.when(s >= dist)
            def _(dist=dist):
                kv_remote(dist, half, head).wait_recv()

        keys = kv[half, head, 0].reshape((NEAR + 1) * HALF, HD)
        values = kv[half, head, 1].reshape((NEAR + 1) * HALF, HD)
        keys_t = keys.T
        causal = key_number + half * HALF <= row_number
        total_k = jnp.zeros(((NEAR + 1) * HALF, HD), F32)
        total_v = jnp.zeros(((NEAR + 1) * HALF, HD), F32)
        last = NEAR * HALF
        for i in range(GROUP):
            at = pl.ds(pl.multiple_of(head * (GROUP * HD) + i * HD, HD), HD)
            q_head = q[:, at]
            g_head = g[:, at]
            number = head * GROUP + i
            scores = dot(keys, q_head, 1, 1)
            scores = jnp.concatenate(
                [jnp.where(causal, scores[0:HALF], scores[last:]), scores[HALF:last]], axis=0
            )
            prob = jnp.exp2(scores * (SCALE * LOG2E) - norm[number][0:1] + bias[half])
            grad_prob = dot(values, g_head, 1, 1)
            grad_prob = jnp.concatenate(
                [jnp.where(causal, grad_prob[0:HALF], grad_prob[last:]), grad_prob[HALF:last]], axis=0
            )
            grad_score = prob * (grad_prob - delta[number][0:1])

            def apart(array):
                first = array[0:HALF]
                return jnp.concatenate(
                    [
                        jnp.where(causal, first, 0.0).astype(BF),
                        array[HALF:last].astype(BF),
                        jnp.where(causal, 0.0, first).astype(BF),
                    ],
                    axis=0,
                )

            prob = apart(prob)
            grad_score = apart(grad_score)
            total_v = total_v + dot(prob, g_head, 1, 0)
            total_k = total_k + dot(grad_score, q_head, 1, 0)
            grad_q = dot(keys_t, grad_score, 1, 0)
            if half == 0:
                dqt[number] = grad_q
            else:
                dq[:, at] = ((dqt[number] + grad_q) * SCALE).T.astype(BF)
            if i == GROUP // 2 - 1:
                middle()
        total_k = total_k * SCALE
        own[half, head, 0] = total_k[0:HALF]
        own[half, head, 1] = total_v[0:HALF]
        for dist in range(1, NEAR + 1):
            part_out[half, head, dist - 1, 0] = total_k[dist * HALF : (dist + 1) * HALF].astype(BF)
            part_out[half, head, dist - 1, 1] = total_v[dist * HALF : (dist + 1) * HALF].astype(BF)

            @pl.when(s >= dist)
            def _(dist=dist):
                part_remote(dist, half, head).start()

    def first_half(head, carry):
        def middle():
            @pl.when(head > 0)
            def _():
                finalize(0, head - 1)

        attend(0, head, middle)
        return carry

    lax.fori_loop(0, KVH, first_half, 0)

    for block in range(16):
        xb_copy(block).wait()
        xb_remote(block).wait_recv()

    def second_half(head, carry):
        def middle():
            @pl.when(head == 0)
            def _():
                finalize(0, KVH - 1)
                input_grad(0)

            @pl.when(head > 0)
            def _():
                finalize(1, head - 1)

        attend(1, head, middle)

        @pl.when(head > 0)
        def _():
            weight_terms(head - 1)

        @pl.when(head > 1)
        def _():
            weight_sums(head - 2)

        return carry

    lax.fori_loop(0, KVH, second_half, 0)
    store_dq = pltpu.make_async_copy(dq, dq_hbm, out_sem.at[0])
    store_dq.start()
    finalize(1, KVH - 1)
    input_grad(1)
    weight_terms(KVH - 1)
    weight_sums(KVH - 2)
    weight_sums(KVH - 1)

    def finish(head, carry):
        weight_final(head)
        return carry

    lax.fori_loop(0, KVH, finish, 0)
    store_gk = pltpu.make_async_copy(gk, gk_hbm, out_sem.at[1])
    store_gv = pltpu.make_async_copy(gv, gv_hbm, out_sem.at[2])
    store_gk.start()
    store_gv.start()

    for half in range(2):

        def sent(head, carry, half=half):
            for dist in range(1, NEAR + 1):

                @pl.when(s + dist <= 7)
                def _(dist=dist):
                    kv_remote(dist, half, head).wait_send()

                @pl.when(s >= dist)
                def _(dist=dist):
                    part_remote(dist, half, head).wait_send()

            pair_remote(half, head).wait_send()

            @pl.when(p > 0)
            def _():
                z_remote(half, head).wait_send()

            @pl.when(p < 3)
            def _():
                z_remote(half, head).wait_recv()

            return carry

        lax.fori_loop(0, 4, sent, 0)

    def sums_sent(head, carry):
        for step in range(1, 4):
            x_first(head, step).wait_send()
            y_first(head, step).wait_send()
            x_second(head, step).wait_send()
            y_second(head, step).wait_send()
        return carry

    lax.fori_loop(0, KVH, sums_sent, 0)
    for block in range(16):
        xb_remote(block).wait_send()
    store_dq.wait()
    store_gk.wait()
    store_gv.wait()


def shards(
    layer_input, queries, keys, values, attn_out, out_grad, log_norm, segment_ids, key_weight, value_weight
):
    any_space = pl.BlockSpec(memory_space=pl.ANY)
    vmem = pltpu.VMEM
    dma = pltpu.SemaphoreType.DMA
    pieces = (2, KVH, NEAR, 2, HALF, HD)
    outs = pl.pallas_call(
        kernel,
        out_shape=(
            jax.ShapeDtypeStruct((TOK, D), BF),
            jax.ShapeDtypeStruct((TOK, D), BF),
            jax.ShapeDtypeStruct((128, KVH * HD), F32),
            jax.ShapeDtypeStruct((128, KVH * HD), F32),
        ),
        in_specs=[any_space] * 10,
        out_specs=(any_space,) * 4,
        scratch_shapes=[
            vmem((TOK, D), BF),
            vmem((TOK, D), BF),
            vmem((TOK, D), BF),
            vmem((TOK, HQ), BF),
            vmem((1, 8 * TOK), jnp.int32),
            vmem((D, KVH * HD), BF),
            vmem((D, KVH * HD), BF),
            vmem((2, KVH, 2, NEAR + 1, HALF, HD), BF),
            vmem((HQ, 8, TOK), F32),
            vmem((HQ, 8, TOK), F32),
            vmem((2, NEAR * HALF, TOK), F32),
            vmem((HQ, HD, TOK), F32),
            vmem((TOK, D), BF),
            vmem(pieces, BF),
            vmem(pieces, BF),
            vmem((2, KVH, 2, HALF, HD), F32),
            vmem((2, HALF, 2 * KVH * HD), BF),
            vmem((KVH, 2, 2, HALF, 2 * HD), BF),
            vmem((2, TOK, 2048), BF),
            vmem((TOK, D), BF),
            vmem((TOK, D), BF),
            vmem((KVH, 3, 4, HD, HD), BF),
            vmem((KVH, 3, 4, HD, HD), BF),
            vmem((KVH, 3, 4, HD, HD), BF),
            vmem((KVH, 3, 4, HD, HD), BF),
            vmem((KVH, 4, HD, HD), F32),
            vmem((KVH, 4, HD, HD), F32),
            vmem((KVH, 3, HD, HD), BF),
            vmem((KVH, 3, HD, HD), BF),
            vmem((KVH, 3, HD, HD), BF),
            vmem((KVH, 3, HD, HD), BF),
            vmem((KVH, HD, HD), F32),
            vmem((KVH, HD, HD), F32),
            vmem((128, KVH * HD), F32),
            vmem((128, KVH * HD), F32),
            dma((7,)),
            dma((2, KVH, 2)),
            dma((16,)),
            dma((16,)),
            dma((16,)),
            dma((NEAR, 2, KVH)),
            dma((NEAR, 2, KVH)),
            dma((NEAR, 2, KVH)),
            dma((NEAR, 2, KVH)),
            dma((2, KVH)),
            dma((2, KVH)),
            dma((2, 4)),
            dma((2, 4)),
        ]
        + [dma((KVH, 3))] * 8
        + [dma((4,))],
        compiler_params=pltpu.CompilerParams(
            collective_id=0, has_side_effects=True, vmem_limit_bytes=60 * 1024 * 1024
        ),
        cost_estimate=pl.CostEstimate(flops=20_000_000_000, bytes_accessed=24_000_000, transcendentals=8_000_000),
        name="attention_backward",
    )(
        layer_input[0, 0], queries[0, 0], keys[0, 0], values[0, 0], attn_out[0, 0], out_grad[0, 0],
        log_norm[0, 0], segment_ids[0], key_weight[0], value_weight[0],
    )
    query_grad, upstream, grad_wk, grad_wv = outs
    return (query_grad[None, None], upstream[None, None], grad_wk[None], grad_wv[None])


def solution(mesh):
    rows = P("dp", "pipe", "seq", None)
    weight = P("pipe", None, None)
    return jax.shard_map(
        shards,
        mesh=mesh,
        in_specs=(rows,) * 7 + (P("dp", "pipe", None), weight, weight),
        out_specs=(rows, rows, P("pipe", ("dp", "seq"), None), P("pipe", ("dp", "seq"), None)),
        check_vma=False,
    )
```

time: 1130 us -> 138 us (0.12)
  waiting for transfers between devices: 537 us -> 0 us
  local copies, waits for them, and re-layouts: 313 us -> 7.46 us
  matrix products: 151 us -> 0 us
  Pallas kernels: 0 us -> 130 us
  blocking collectives: 44.4 us -> 0 us
  starting transfers between devices: 26.9 us -> 0 us
  loops' own time: 26.7 us -> 0 us
  between operations: 14.3 us -> 0.65 us
    reduce_scatter x4 -> x0, waiting for transfers between devices: 432 us -> none  [the longest x1 167 us: shards(): lax.psum_scatter(local_wk, ('dp', 'seq'), scatter_dimension=0, tiled=True)]
    dynamic_update_slice x16 -> x0, local copies, waits for them, and re-layouts: 229 us -> none  [shards(): lax.map(one_head, jnp.arange(local_heads, dtype=jnp.int32))]
    dot_general x86 -> x0, matrix products: 151 us -> none  [the longest x16 41.9 us: attend(): lax.dot_general(query_block, head_keys, (((1,), (1,)), ((), ())), preferr...]
    pallas_call x0 -> x1, Pallas kernels: none -> 130 us  [shards(): pl.pallas_call(kernel, out_shape=(jax.ShapeDtypeStruct((TOK, D), BF), jax...]
    all_to_all x4 -> x0, waiting for transfers between devices: 58 us -> none  [the longest x1 27.6 us: shards(): lax.all_to_all(grad_rows, 'seq', split_axis=1, concat_axis=0, tiled=True)]
    all_gather x2 -> x0, waiting for transfers between devices: 45.2 us -> none  [the longest x1 45.2 us: shards(): lax.all_gather(value_rows, 'seq', axis=0, tiled=True)]
    all_to_all x1 -> x0, blocking collectives: 44.4 us -> none  [shards(): lax.all_to_all(head_dq, 'seq', split_axis=0, concat_axis=1, tiled=True)]
    dynamic_slice x64 -> x0, local copies, waits for them, and re-layouts: 33.9 us -> none  [the longest x20 13 us: shards(): lax.map(one_head, jnp.arange(local_heads, dtype=jnp.int32))]
  transfers between devices with their start and end apart: 11 -> 0, of which waited for: 8 -> 0; matrix products, arithmetic and copies ran while one was open for 5% -> 0% of each run, Pallas kernels for 0% -> 0%
where the time goes in v1:
time: 138 us
  Pallas kernels  130 us (94%)
  local copies, waits for them, and re-layouts  7.46 us (5%)
    pallas_call x1, Pallas kernels, shards(): pl.pallas_call(kernel, out_shape=(jax.ShapeDtypeStruct((TOK, D), BF), jax...  130 us
    unnamed x11, local copies, waits for them, and re-layouts  7.46 us

profile of v1, /device:TPU:0, one launch (start us, length us, event | category | flops | bytes accessed | tf_op | source)
XLA Modules:
  0.0 137.7 jit_solution(16128080147205211158)
XLA Ops:
  0.6 1.5 %copy.14 = bf16[1,1,256,32]{3,2,1,0:T(8,128)(2,1)} copy(bf16[1,1,256,32]{2,3,1,0:T(8,128)(2,1)} %param.16) | data formatting | bytes 32768 | tf_op args[6]
  2.1 129.6 %attention_backward.1 = (bf16[256,4096]{1,0:T(8,128)(2,1)}, bf16[256,4096]{1,0:T(8,128)(2,1)}, f32[128,512]{1,0:T(8,128)}, f32[128,512]{1,0:T(8,128)}) custom-call(bf16[256,4096]{1,0:T(8,128)(2,1)} %bitcast.21, bf16[256,4096]{1,0:T(8,128)(2,1)} %bitcast.22, bf16[256,512]{1,0:T(8,128)(2,1)} %bitcast.25, bf16[256,512]{1,0:T(8,128)(2,1)} %bitcast.26, ...), custom_call_target="tpu_custom_call" | custom-call | flops 20000000000 | bytes 24000000 | tf_op jit(solution)/shard_map/attention_backward/pallas_call | solution.py:501
  131.7 0.0 copy-start
  131.7 3.3 %copy.19 = bf16[1,1,256,4096]{3,2,1,0:T(8,128)(2,1)} copy(bf16[1,1,256,4096]{3,2,1,0:T(8,128)(2,1)} %bitcast.15) | data formatting | bytes 4194304
  135.0 0.0 copy-done
  135.0 0.0 copy-start.2
  135.0 0.0 copy-start.1
  135.0 1.3 copy.20
  136.3 0.0 copy-done.2
  136.3 0.7 copy.21
  137.0 0.0 copy-done.1
  137.0 0.7 copy.22
Async XLA Ops:
  131.7 3.3 %copy-start = (bf16[256,4096]{1,0:T(8,128)(2,1)S(1)}, bf16[256,4096]{1,0:T(8,128)(2,1)}, u32[]{:S(2)}) copy-start(bf16[256,4096]{1,0:T(8,128)(2,1)} %get-tuple-element.9) | copy-start | bytes 6291460
  135.0 1.3 copy-start.2
  135.0 2.0 %copy-start.1 = (f32[128,512]{1,0:T(8,128)S(1)}, f32[128,512]{1,0:T(8,128)}, u32[]{:S(2)}) copy-start(f32[128,512]{1,0:T(8,128)} %get-tuple-element.11) | copy-start | bytes 786436

commit v2 on v1

--- a/solution.py
+++ b/solution.py
@@ -32,7 +32,7 @@
     x_hbm, q_hbm, k_hbm, v_hbm, o_hbm, g_hbm, norm_hbm, seg_hbm, wk_hbm, wv_hbm,
     dq_hbm, up_hbm, gk_hbm, gv_hbm,
     q, g, o, norm_in, seg, wk, wv, kv, norm, delta, bias, dqt, dq,
-    part_out, part_in, own, grads, pair, xb, up, zeros,
+    part_out, part_in, relay, own, grads, pair, xb, up, z_pass, zeros,
     xs_out, xs_in, ys_out, ys_in, x_own, y_own, x2_out, x2_in, y2_out, y2_in, x_fin, y_fin, gk, gv,
     in_sem, kv_local, xb_local, xb_send, xb_recv, kv_send, kv_recv, part_send, part_recv,
     pair_send, pair_recv, z_send, z_recv, xs_send, xs_recv, ys_send, ys_recv,
@@ -77,7 +77,7 @@
             ((norm_hbm, norm_in), (seg_hbm, seg), (g_hbm, g), (o_hbm, o), (q_hbm, q), (wk_hbm, wk), (wv_hbm, wv))
         )
     ]
-    for copy in loads:
+    for copy in loads[:5]:
         copy.start()
 
     def x_columns(block, owner_core):
@@ -101,23 +101,26 @@
             device_id_type=MESH,
         )
 
-    def kv_remote(dist, half, head):
+    def in_row(step):
+        return (dp, p, y_hi * 4 + lax.rem(x_at + step, 4))
+
+    def kv_remote(dist, half, head, which=0, source=0):
         return pltpu.make_async_remote_copy(
-            src_ref=kv.at[half, head, :, 0],
-            dst_ref=kv.at[half, head, :, dist],
-            send_sem=kv_send.at[dist - 1, half, head],
-            recv_sem=kv_recv.at[dist - 1, half, head],
-            device_id=(dp, p, lax.rem(s + dist, 8)),
+            src_ref=kv.at[half, head, which, source],
+            dst_ref=kv.at[half, head, which, dist],
+            send_sem=kv_send.at[which, dist - 1, half, head],
+            recv_sem=kv_recv.at[which, dist - 1, half, head],
+            device_id=in_row(dist) if dist < NEAR and which == 0 else (dp, p, lax.rem(s + dist, 8)),
             device_id_type=MESH,
         )
 
-    def part_remote(dist, half, head):
+    def part_remote(dist, half, head, which=0):
         return pltpu.make_async_remote_copy(
-            src_ref=part_out.at[half, head, dist - 1],
-            dst_ref=part_in.at[half, head, dist - 1],
-            send_sem=part_send.at[dist - 1, half, head],
-            recv_sem=part_recv.at[dist - 1, half, head],
-            device_id=(dp, p, lax.rem(s + 8 - dist, 8)),
+            src_ref=part_out.at[half, head, dist - 1, which],
+            dst_ref=part_in.at[half, head, dist - 1, which],
+            send_sem=part_send.at[which, dist - 1, half, head],
+            recv_sem=part_recv.at[which, dist - 1, half, head],
+            device_id=in_row(4 - dist) if dist < NEAR and which == 0 else (dp, p, lax.rem(s + 8 - dist, 8)),
             device_id_type=MESH,
         )
 
@@ -131,15 +134,29 @@
             device_id_type=MESH,
         )
 
-    def z_remote(half, chunk):
+    def z_remote(half, chunk, hop=0):
+        rows = pl.ds(half * HALF, HALF)
+        at = pl.ds(pl.multiple_of(chunk * 1024, 1024), 1024)
+        if isinstance(chunk, int) and chunk == 3:
+            source = (up.at[rows, at], z_pass.at[half, 0], z_pass.at[half, 1])[hop]
+            target = (z_pass.at[half, 0], z_pass.at[half, 1], up_hbm.at[rows, at])[hop]
+            to, number = lax.rem(p + 1, 4), 3 + hop
+        else:
+            source, target, to, number = up.at[rows, at], up_hbm.at[rows, at], lax.rem(p + 3, 4), chunk
         return pltpu.make_async_remote_copy(
-            src_ref=up.at[pl.ds(half * HALF, HALF), pl.ds(chunk * 1024, 1024)],
-            dst_ref=up_hbm.at[pl.ds(half * HALF, HALF), pl.ds(chunk * 1024, 1024)],
-            send_sem=z_send.at[half, chunk],
-            recv_sem=z_recv.at[half, chunk],
-            device_id=(dp, lax.rem(p + 3, 4), s),
+            src_ref=source,
+            dst_ref=target,
+            send_sem=z_send.at[half, number],
+            recv_sem=z_recv.at[half, number],
+            device_id=(dp, to, s),
             device_id_type=MESH,
         )
+
+    def pass_z(half, hop):
+        @pl.when(p != hop)
+        def _():
+            z_remote(half, 3, hop - 1).wait_recv()
+            z_remote(half, 3, hop).start()
 
     def spread(source, target, send, recv, reach, head, step):
         return pltpu.make_async_remote_copy(
@@ -166,28 +183,45 @@
         copy.wait()
     pl.semaphore_wait(barrier, len(peers))
 
+    def send_kv(half, head):
+        @pl.when(s < NEAR)
+        def _():
+            kv_remote(NEAR, half, head).start()
+
+        for dist in range(1, NEAR):
+
+            @pl.when(x_at + dist < 4)
+            def _(dist=dist):
+                kv_remote(dist, half, head).start()
+
+        for dist in range(1, NEAR + 1):
+
+            @pl.when(s + dist <= 7)
+            def _(dist=dist):
+                kv_remote(dist, half, head, 1).start()
+
+    def pass_kv(half, head):
+        @pl.when(s >= NEAR)
+        def _():
+            kv_remote(NEAR, half, head).wait_recv()
+            for dist in range(1, NEAR):
+
+                @pl.when(x_at + dist >= 4)
+                def _(dist=dist):
+                    kv_remote(dist, half, head, 0, NEAR).start()
+
+    send_kv(0, 0)
     for half in range(2):
         for head in range(KVH):
             for dist in range(1, NEAR + 1):
 
-                @pl.when(s + dist <= 7)
-                def _(dist=dist, half=half, head=head):
-                    kv_remote(dist, half, head).start()
-
                 @pl.when(s < dist)
                 def _(dist=dist, half=half, head=head):
                     kv[half, head, :, dist] = jnp.zeros((2, HALF, HD), BF)
 
-    for block in range(16):
-        xb_copy(block).start()
-        xb_remote(block).start()
-
     loads[0].wait()
     loads[1].wait()
-    eye = (
-        lax.broadcasted_iota(jnp.int32, (HQ, HQ), 0) == lax.broadcasted_iota(jnp.int32, (HQ, HQ), 1)
-    ).astype(F32).astype(BF)
-    norm_rows = dot(eye, norm_in[...], 1, 1) * LOG2E
+    norm_rows = norm_in[...].astype(F32) * LOG2E
     for head in range(HQ):
         norm[head] = jnp.broadcast_to(norm_rows[head : head + 1], (8, TOK))
 
@@ -206,8 +240,8 @@
 
     for half in range(2):
         causal = key_number + half * HALF <= row_number
-        bias[half, 0:HALF] = jnp.where(causal, document_bias(0, half), document_bias(NEAR, half))
-        for dist in range(1, NEAR):
+        bias[half, 0:HALF] = jnp.where(causal, document_bias(0, half), MASKED)
+        for dist in range(1, NEAR + 1):
             bias[half, dist * HALF : (dist + 1) * HALF] = document_bias(dist, half)
 
     loads[2].wait()
@@ -226,22 +260,48 @@
         return carry
 
     lax.fori_loop(0, HQ, delta_head, 0, unroll=4)
+    send_kv(0, 1)
+    pass_kv(0, 0)
     loads[4].wait()
+    loads[5].start()
+    loads[6].start()
+    for block in range(16):
+        xb_copy(block).start()
+        xb_remote(block).start()
+
+    def fill():
+        return pltpu.make_async_copy(zeros, up_hbm, out_sem.at[3])
 
     @pl.when(p == 3)
     def _():
         zeros[...] = jnp.zeros((TOK, D), BF)
-        fill = pltpu.make_async_copy(zeros, up_hbm, out_sem.at[3])
-        fill.start()
-        fill.wait()
+        fill().start()
+
+    def pass_part(half, head):
+        @pl.when(s >= NEAR)
+        def _():
+            for dist in range(1, NEAR):
+
+                @pl.when(x_at + dist >= 4)
+                def _(dist=dist):
+                    part_remote(dist, half, head).wait_recv()
+                    relay[half, head] += part_in[half, head, dist - 1, 0].astype(F32)
+
+            part_out[half, head, NEAR - 1, 0] = relay[half, head].astype(BF)
+            part_remote(NEAR, half, head).start()
 
     def finalize(half, head):
         for dist in range(1, NEAR + 1):
 
+            @pl.when(x_at + dist < 4 if dist < NEAR else s < NEAR)
+            def _(dist=dist):
+                part_remote(dist, half, head).wait_recv()
+                own[half, head, 0] += part_in[half, head, dist - 1, 0].astype(F32)
+
             @pl.when(s + dist <= 7)
             def _(dist=dist):
-                part_remote(dist, half, head).wait_recv()
-                own[half, head] += part_in[half, head, dist - 1].astype(F32)
+                part_remote(dist, half, head, 1).wait_recv()
+                own[half, head, 1] += part_in[half, head, dist - 1, 1].astype(F32)
 
         total = own[half, head].astype(BF)
         at = pl.multiple_of(head * HD, HD)
@@ -257,7 +317,7 @@
             loads[6].wait()
         rows = pl.ds(half * HALF, HALF)
 
-        def chunk_step(chunk, carry):
+        def columns(chunk):
             for part in range(2):
                 at = pl.ds(pl.multiple_of(chunk * 1024 + part * 512, 512), 512)
                 total = dot(grads[half, :, 0 : KVH * HD], wk[at, :], 1, 1)
@@ -268,9 +328,12 @@
             def _():
                 z_remote(half, chunk).start()
 
+        def chunk_step(chunk, carry):
+            columns(chunk)
             return carry
 
-        lax.fori_loop(0, 4, chunk_step, 0)
+        columns(3)
+        lax.fori_loop(0, 3, chunk_step, 0)
 
     def weight_terms(head):
         pair_remote(0, head).wait_recv()
@@ -328,76 +391,76 @@
         gk[:, at] = total.T
         gv[:, at] = other.T
 
-    def attend(half, head, middle):
-        for dist in range(1, NEAR + 1):
+    def attend(half, head):
+        for dist in range(1, NEAR):
 
             @pl.when(s >= dist)
             def _(dist=dist):
                 kv_remote(dist, half, head).wait_recv()
 
+        for dist in range(1, NEAR + 1):
+
+            @pl.when(s >= dist)
+            def _(dist=dist):
+                kv_remote(dist, half, head, 1).wait_recv()
+
         keys = kv[half, head, 0].reshape((NEAR + 1) * HALF, HD)
         values = kv[half, head, 1].reshape((NEAR + 1) * HALF, HD)
         keys_t = keys.T
-        causal = key_number + half * HALF <= row_number
         total_k = jnp.zeros(((NEAR + 1) * HALF, HD), F32)
         total_v = jnp.zeros(((NEAR + 1) * HALF, HD), F32)
-        last = NEAR * HALF
         for i in range(GROUP):
             at = pl.ds(pl.multiple_of(head * (GROUP * HD) + i * HD, HD), HD)
             q_head = q[:, at]
             g_head = g[:, at]
             number = head * GROUP + i
             scores = dot(keys, q_head, 1, 1)
-            scores = jnp.concatenate(
-                [jnp.where(causal, scores[0:HALF], scores[last:]), scores[HALF:last]], axis=0
-            )
             prob = jnp.exp2(scores * (SCALE * LOG2E) - norm[number][0:1] + bias[half])
             grad_prob = dot(values, g_head, 1, 1)
-            grad_prob = jnp.concatenate(
-                [jnp.where(causal, grad_prob[0:HALF], grad_prob[last:]), grad_prob[HALF:last]], axis=0
-            )
-            grad_score = prob * (grad_prob - delta[number][0:1])
-
-            def apart(array):
-                first = array[0:HALF]
-                return jnp.concatenate(
-                    [
-                        jnp.where(causal, first, 0.0).astype(BF),
-                        array[HALF:last].astype(BF),
-                        jnp.where(causal, 0.0, first).astype(BF),
-                    ],
-                    axis=0,
-                )
-
-            prob = apart(prob)
-            grad_score = apart(grad_score)
-            total_v = total_v + dot(prob, g_head, 1, 0)
+            grad_score = (prob * (grad_prob - delta[number][0:1])).astype(BF)
+            total_v = total_v + dot(prob.astype(BF), g_head, 1, 0)
             total_k = total_k + dot(grad_score, q_head, 1, 0)
             grad_q = dot(keys_t, grad_score, 1, 0)
             if half == 0:
                 dqt[number] = grad_q
             else:
                 dq[:, at] = ((dqt[number] + grad_q) * SCALE).T.astype(BF)
-            if i == GROUP // 2 - 1:
-                middle()
         total_k = total_k * SCALE
         own[half, head, 0] = total_k[0:HALF]
         own[half, head, 1] = total_v[0:HALF]
+        relay[half, head] = total_k[NEAR * HALF :]
         for dist in range(1, NEAR + 1):
-            part_out[half, head, dist - 1, 0] = total_k[dist * HALF : (dist + 1) * HALF].astype(BF)
-            part_out[half, head, dist - 1, 1] = total_v[dist * HALF : (dist + 1) * HALF].astype(BF)
+            rows = slice(dist * HALF, (dist + 1) * HALF)
+            if dist < NEAR:
+                part_out[half, head, dist - 1, 0] = total_k[rows].astype(BF)
+            part_out[half, head, dist - 1, 1] = total_v[rows].astype(BF)
 
             @pl.when(s >= dist)
             def _(dist=dist):
-                part_remote(dist, half, head).start()
+                if dist < NEAR:
+                    part_remote(dist, half, head).start()
+                part_remote(dist, half, head, 1).start()
 
     def first_half(head, carry):
-        def middle():
-            @pl.when(head > 0)
-            def _():
-                finalize(0, head - 1)
-
-        attend(0, head, middle)
+        @pl.when(head < 2)
+        def _():
+            send_kv(0, head + 2)
+
+        @pl.when(head >= 2)
+        def _():
+            send_kv(1, head - 2)
+            pass_part(0, head - 2)
+
+        @pl.when(head < 3)
+        def _():
+            pass_kv(0, head + 1)
+
+        @pl.when(head == 3)
+        def _():
+            pass_kv(1, 0)
+            finalize(0, 0)
+
+        attend(0, head)
         return carry
 
     lax.fori_loop(0, KVH, first_half, 0)
@@ -407,36 +470,51 @@
         xb_remote(block).wait_recv()
 
     def second_half(head, carry):
-        def middle():
-            @pl.when(head == 0)
-            def _():
-                finalize(0, KVH - 1)
-                input_grad(0)
-
-            @pl.when(head > 0)
-            def _():
-                finalize(1, head - 1)
-
-        attend(1, head, middle)
-
-        @pl.when(head > 0)
-        def _():
-            weight_terms(head - 1)
-
-        @pl.when(head > 1)
-        def _():
-            weight_sums(head - 2)
-
+        @pl.when(head < 2)
+        def _():
+            send_kv(1, head + 2)
+            pass_part(0, head + 2)
+
+        @pl.when(head >= 2)
+        def _():
+            pass_part(1, head - 2)
+
+        @pl.when(head < 3)
+        def _():
+            pass_kv(1, head + 1)
+            finalize(0, head + 1)
+
+        @pl.when(head == 2)
+        def _():
+            input_grad(0)
+
+        @pl.when(head == 3)
+        def _():
+            finalize(1, 0)
+
+        attend(1, head)
         return carry
 
     lax.fori_loop(0, KVH, second_half, 0)
     store_dq = pltpu.make_async_copy(dq, dq_hbm, out_sem.at[0])
     store_dq.start()
-    finalize(1, KVH - 1)
+    pass_part(1, 2)
+    pass_z(0, 1)
+    finalize(1, 1)
+    weight_terms(0)
+    pass_part(1, 3)
+    finalize(1, 2)
+    weight_terms(1)
+    finalize(1, 3)
     input_grad(1)
-    weight_terms(KVH - 1)
-    weight_sums(KVH - 2)
-    weight_sums(KVH - 1)
+    pass_z(0, 2)
+    weight_terms(2)
+    weight_terms(3)
+    weight_sums(0)
+    weight_sums(1)
+    pass_z(1, 1)
+    weight_sums(2)
+    weight_sums(3)
 
     def finish(head, carry):
         weight_final(head)
@@ -447,13 +525,14 @@
     store_gv = pltpu.make_async_copy(gv, gv_hbm, out_sem.at[2])
     store_gk.start()
     store_gv.start()
+    pass_z(1, 2)
 
     for half in range(2):
 
         def sent(head, carry, half=half):
-            for dist in range(1, NEAR + 1):
-
-                @pl.when(s + dist <= 7)
+            for dist in range(1, NEAR):
+
+                @pl.when(jnp.logical_or(x_at + dist < 4, s >= NEAR))
                 def _(dist=dist):
                     kv_remote(dist, half, head).wait_send()
 
@@ -461,15 +540,25 @@
                 def _(dist=dist):
                     part_remote(dist, half, head).wait_send()
 
+            for dist in range(1, NEAR + 1):
+
+                @pl.when(s + dist <= 7)
+                def _(dist=dist):
+                    kv_remote(dist, half, head, 1).wait_send()
+
+                @pl.when(s >= dist)
+                def _(dist=dist):
+                    part_remote(dist, half, head, 1).wait_send()
+
+            @pl.when(s < NEAR)
+            def _():
+                kv_remote(NEAR, half, head).wait_send()
+
+            @pl.when(s >= NEAR)
+            def _():
+                part_remote(NEAR, half, head).wait_send()
+
             pair_remote(half, head).wait_send()
-
-            @pl.when(p > 0)
-            def _():
-                z_remote(half, head).wait_send()
-
-            @pl.when(p < 3)
-            def _():
-                z_remote(half, head).wait_recv()
 
             return carry
 
@@ -484,11 +573,42 @@
         return carry
 
     lax.fori_loop(0, KVH, sums_sent, 0)
+    for half in range(2):
+
+        @pl.when(p > 0)
+        def _(half=half):
+            for chunk in range(4):
+                z_remote(half, chunk).wait_send()
+
+        for hop in (1, 2):
+
+            @pl.when(p != hop)
+            def _(half=half, hop=hop):
+                z_remote(half, 3, hop).wait_send()
+
+        @pl.when(p < 3)
+        def _(half=half):
+            for chunk in range(3):
+                z_remote(half, chunk).wait_recv()
+            z_remote(half, 3, 2).wait_recv()
+
     for block in range(16):
         xb_remote(block).wait_send()
+
+    @pl.when(p == 3)
+    def _():
+        fill().wait()
+
     store_dq.wait()
     store_gk.wait()
     store_gv.wait()
+
+
+def hand_out(dq, up, gk, gv, dq_out, up_out, gk_out, gv_out):
+    dq_out[...] = dq[...]
+    up_out[...] = up[...]
+    gk_out[...] = gk[...]
+    gv_out[...] = gv[...]
 
 
 def shards(
@@ -498,37 +618,40 @@
     vmem = pltpu.VMEM
     dma = pltpu.SemaphoreType.DMA
     pieces = (2, KVH, NEAR, 2, HALF, HD)
+    out_shape = (
+        jax.ShapeDtypeStruct((TOK, D), BF),
+        jax.ShapeDtypeStruct((TOK, D), BF),
+        jax.ShapeDtypeStruct((128, KVH * HD), F32),
+        jax.ShapeDtypeStruct((128, KVH * HD), F32),
+    )
     outs = pl.pallas_call(
         kernel,
-        out_shape=(
-            jax.ShapeDtypeStruct((TOK, D), BF),
-            jax.ShapeDtypeStruct((TOK, D), BF),
-            jax.ShapeDtypeStruct((128, KVH * HD), F32),
-            jax.ShapeDtypeStruct((128, KVH * HD), F32),
-        ),
+        out_shape=out_shape,
         in_specs=[any_space] * 10,
         out_specs=(any_space,) * 4,
         scratch_shapes=[
             vmem((TOK, D), BF),
             vmem((TOK, D), BF),
             vmem((TOK, D), BF),
-            vmem((TOK, HQ), BF),
+            vmem((HQ, TOK), BF),
             vmem((1, 8 * TOK), jnp.int32),
             vmem((D, KVH * HD), BF),
             vmem((D, KVH * HD), BF),
             vmem((2, KVH, 2, NEAR + 1, HALF, HD), BF),
             vmem((HQ, 8, TOK), F32),
             vmem((HQ, 8, TOK), F32),
-            vmem((2, NEAR * HALF, TOK), F32),
+            vmem((2, (NEAR + 1) * HALF, TOK), F32),
             vmem((HQ, HD, TOK), F32),
             vmem((TOK, D), BF),
             vmem(pieces, BF),
             vmem(pieces, BF),
+            vmem((2, KVH, HALF, HD), F32),
             vmem((2, KVH, 2, HALF, HD), F32),
             vmem((2, HALF, 2 * KVH * HD), BF),
             vmem((KVH, 2, 2, HALF, 2 * HD), BF),
             vmem((2, TOK, 2048), BF),
             vmem((TOK, D), BF),
+            vmem((2, 2, HALF, 1024), BF),
             vmem((TOK, D), BF),
             vmem((KVH, 3, 4, HD, HD), BF),
             vmem((KVH, 3, 4, HD, HD), BF),
@@ -549,14 +672,14 @@
             dma((16,)),
             dma((16,)),
             dma((16,)),
-            dma((NEAR, 2, KVH)),
-            dma((NEAR, 2, KVH)),
-            dma((NEAR, 2, KVH)),
-            dma((NEAR, 2, KVH)),
+            dma((2, NEAR, 2, KVH)),
+            dma((2, NEAR, 2, KVH)),
+            dma((2, NEAR, 2, KVH)),
+            dma((2, NEAR, 2, KVH)),
             dma((2, KVH)),
             dma((2, KVH)),
-            dma((2, 4)),
-            dma((2, 4)),
+            dma((2, 6)),
+            dma((2, 6)),
         ]
         + [dma((KVH, 3))] * 8
         + [dma((4,))],
@@ -567,9 +690,17 @@
         name="attention_backward",
     )(
         layer_input[0, 0], queries[0, 0], keys[0, 0], values[0, 0], attn_out[0, 0], out_grad[0, 0],
-        log_norm[0, 0], segment_ids[0], key_weight[0], value_weight[0],
+        log_norm[0, 0].T, segment_ids[0], key_weight[0], value_weight[0],
     )
-    query_grad, upstream, grad_wk, grad_wv = outs
+    blocks = tuple(pl.BlockSpec((rows // 2, columns), lambda i: (i, 0)) for rows, columns in (o.shape for o in out_shape))
+    query_grad, upstream, grad_wk, grad_wv = pl.pallas_call(
+        hand_out,
+        out_shape=out_shape,
+        grid=(2,),
+        in_specs=blocks,
+        out_specs=blocks,
+        name="hand_out",
+    )(*outs)
     return (query_grad[None, None], upstream[None, None], grad_wk[None], grad_wv[None])
 
 

time: 138 us -> 110 us (0.80)
  Pallas kernels: 130 us -> 109 us
  local copies, waits for them, and re-layouts: 7.46 us -> 0 us
    pallas_call x1 -> x2, Pallas kernels: 130 us -> 109 us  [the longest x1 105 us: shards(): pl.pallas_call(kernel, out_shape=out_shape, in_specs=[any_space] * 10, ou...]
    unnamed x11 -> x0, local copies, waits for them, and re-layouts: 7.46 us -> none
where the time goes in v2:
time: 110 us
  Pallas kernels  109 us (99%)
    pallas_call x1, Pallas kernels, shards(): pl.pallas_call(kernel, out_shape=out_shape, in_specs=[any_space] * 10, ou...  105 us
    pallas_call x1, Pallas kernels, shards(): pl.pallas_call(hand_out, out_shape=out_shape, grid=(2,), in_specs=blocks,...  3.91 us

profile of v2, /device:TPU:0, one launch (start us, length us, event | category | flops | bytes accessed | tf_op | source)
XLA Modules:
  0.0 109.6 jit_solution(4773395488032604295)
XLA Ops:
  0.6 104.9 %attention_backward.1 = (bf16[256,4096]{1,0:T(8,128)(2,1)}, bf16[256,4096]{1,0:T(8,128)(2,1)}, f32[128,512]{1,0:T(8,128)}, f32[128,512]{1,0:T(8,128)}) custom-call(bf16[256,4096]{1,0:T(8,128)(2,1)} %bitcast.18, bf16[256,4096]{1,0:T(8,128)(2,1)} %bitcast.19, bf16[256,512]{1,0:T(8,128)(2,1)} %bitcast.24, bf16[256,512]{1,0:T(8,128)(2,1)} %bitcast.25, ...), custom_call_target="tpu_custom_call" | custom-call | flops 20000000000 | bytes 24000000 | tf_op jit(solution)/shard_map/attention_backward/pallas_call | solution.py:627
  105.6 3.9 %hand_out.1 = (bf16[256,4096]{1,0:T(8,128)(2,1)}, bf16[256,4096]{1,0:T(8,128)(2,1)}, f32[128,512]{1,0:T(8,128)}, f32[128,512]{1,0:T(8,128)}) custom-call(bf16[256,4096]{1,0:T(8,128)(2,1)} %get-tuple-element.12.dq, bf16[256,4096]{1,0:T(8,128)(2,1)} %get-tuple-element.13.up, f32[128,512]{1,0:T(8,128)} %get-tuple-element.14.gk, f32[128,512]{1,0:T(8,128)} %get-tuple-element.15.gv), custom_call_target="tpu_custom_call" | custom-call | tf_op jit(solution)/shard_map/hand_out/pallas_call | solution.py:696

commit v3 on v2

--- a/solution.py
+++ b/solution.py
@@ -262,6 +262,7 @@
     lax.fori_loop(0, HQ, delta_head, 0, unroll=4)
     send_kv(0, 1)
     pass_kv(0, 0)
+    send_kv(0, 2)
     loads[4].wait()
     loads[5].start()
     loads[6].start()
@@ -354,9 +355,10 @@
 
         for ry in range(4):
             row_of_targets(ry)
+            if ry > 0:
+                y_first(head, ry).start()
         for step in range(1, 4):
             x_first(head, step).start()
-            y_first(head, step).start()
 
     def weight_sums(head):
         for step in range(1, 4):
@@ -442,13 +444,16 @@
                 part_remote(dist, half, head, 1).start()
 
     def first_half(head, carry):
-        @pl.when(head < 2)
-        def _():
-            send_kv(0, head + 2)
+        @pl.when(head == 0)
+        def _():
+            send_kv(0, 3)
+
+        @pl.when(head > 0)
+        def _():
+            send_kv(1, head - 1)
 
         @pl.when(head >= 2)
         def _():
-            send_kv(1, head - 2)
             pass_part(0, head - 2)
 
         @pl.when(head < 3)
@@ -470,9 +475,12 @@
         xb_remote(block).wait_recv()
 
     def second_half(head, carry):
+        @pl.when(head == 0)
+        def _():
+            send_kv(1, 3)
+
         @pl.when(head < 2)
         def _():
-            send_kv(1, head + 2)
             pass_part(0, head + 2)
 
         @pl.when(head >= 2)
@@ -499,21 +507,22 @@
     store_dq = pltpu.make_async_copy(dq, dq_hbm, out_sem.at[0])
     store_dq.start()
     pass_part(1, 2)
-    pass_z(0, 1)
     finalize(1, 1)
     weight_terms(0)
+    pass_z(0, 1)
     pass_part(1, 3)
     finalize(1, 2)
     weight_terms(1)
     finalize(1, 3)
     input_grad(1)
-    pass_z(0, 2)
     weight_terms(2)
     weight_terms(3)
+    pass_z(0, 2)
     weight_sums(0)
+    pass_z(1, 1)
     weight_sums(1)
-    pass_z(1, 1)
     weight_sums(2)
+    pass_z(1, 2)
     weight_sums(3)
 
     def finish(head, carry):
@@ -525,7 +534,6 @@
     store_gv = pltpu.make_async_copy(gv, gv_hbm, out_sem.at[2])
     store_gk.start()
     store_gv.start()
-    pass_z(1, 2)
 
     for half in range(2):
 
@@ -604,11 +612,26 @@
     store_gv.wait()
 
 
-def hand_out(dq, up, gk, gv, dq_out, up_out, gk_out, gv_out):
-    dq_out[...] = dq[...]
-    up_out[...] = up[...]
-    gk_out[...] = gk[...]
-    gv_out[...] = gv[...]
+def hand_out(dq, up, gk, gv, dq_out, up_out, gk_out, gv_out, dq_held, up_held, gk_held, gv_held, into, out):
+    pieces = []
+    for source, held, target, parts in (
+        (dq, dq_held, dq_out, 4), (up, up_held, up_out, 4), (gk, gk_held, gk_out, 1), (gv, gv_held, gv_out, 1)
+    ):
+        size = source.shape[0] // parts
+        for part in range(parts):
+            rows = pl.ds(part * size, size)
+            number = len(pieces)
+            pieces.append((
+                pltpu.make_async_copy(source.at[rows], held.at[rows], into.at[number]),
+                pltpu.make_async_copy(held.at[rows], target.at[rows], out.at[number]),
+            ))
+    for first, _ in pieces:
+        first.start()
+    for first, second in pieces:
+        first.wait()
+        second.start()
+    for _, second in pieces:
+        second.wait()
 
 
 def shards(
@@ -692,13 +715,12 @@
         layer_input[0, 0], queries[0, 0], keys[0, 0], values[0, 0], attn_out[0, 0], out_grad[0, 0],
         log_norm[0, 0].T, segment_ids[0], key_weight[0], value_weight[0],
     )
-    blocks = tuple(pl.BlockSpec((rows // 2, columns), lambda i: (i, 0)) for rows, columns in (o.shape for o in out_shape))
     query_grad, upstream, grad_wk, grad_wv = pl.pallas_call(
         hand_out,
         out_shape=out_shape,
-        grid=(2,),
-        in_specs=blocks,
-        out_specs=blocks,
+        in_specs=[any_space] * 4,
+        out_specs=(any_space,) * 4,
+        scratch_shapes=[vmem(o.shape, o.dtype) for o in out_shape] + [dma((10,)), dma((10,))],
         name="hand_out",
     )(*outs)
     return (query_grad[None, None], upstream[None, None], grad_wk[None], grad_wv[None])

time: 110 us -> 109 us (level)
    pallas_call x1, Pallas kernels: 105 us -> 104 us  [shards(): pl.pallas_call(kernel, out_shape=out_shape, in_specs=[any_space] * 10, ou...]
where the time goes in v3:
time: 109 us; the launch traced here: 108 us
  Pallas kernels  108 us (99%)
    pallas_call x1, Pallas kernels, shards(): pl.pallas_call(kernel, out_shape=out_shape, in_specs=[any_space] * 10, ou...  104 us
    pallas_call x1, Pallas kernels, shards(): pl.pallas_call(hand_out, out_shape=out_shape, in_specs=[any_space] * 4, o...  4.07 us

profile of v3, /device:TPU:0, one launch (start us, length us, event | category | flops | bytes accessed | tf_op | source)
XLA Modules:
  0.0 108.4 jit_solution(11777490782262310251)
XLA Ops:
  0.6 103.5 %attention_backward.1 = (bf16[256,4096]{1,0:T(8,128)(2,1)}, bf16[256,4096]{1,0:T(8,128)(2,1)}, f32[128,512]{1,0:T(8,128)}, f32[128,512]{1,0:T(8,128)}) custom-call(bf16[256,4096]{1,0:T(8,128)(2,1)} %bitcast.18, bf16[256,4096]{1,0:T(8,128)(2,1)} %bitcast.19, bf16[256,512]{1,0:T(8,128)(2,1)} %bitcast.24, bf16[256,512]{1,0:T(8,128)(2,1)} %bitcast.25, ...), custom_call_target="tpu_custom_call" | custom-call | flops 20000000000 | bytes 24000000 | tf_op jit(solution)/shard_map/attention_backward/pallas_call | solution.py:650
  104.2 4.1 %hand_out.1 = (bf16[256,4096]{1,0:T(8,128)(2,1)}, bf16[256,4096]{1,0:T(8,128)(2,1)}, f32[128,512]{1,0:T(8,128)}, f32[128,512]{1,0:T(8,128)}) custom-call(bf16[256,4096]{1,0:T(8,128)(2,1)} %get-tuple-element.12.dq, bf16[256,4096]{1,0:T(8,128)(2,1)} %get-tuple-element.13.up, f32[128,512]{1,0:T(8,128)} %get-tuple-element.14.gk, f32[128,512]{1,0:T(8,128)} %get-tuple-element.15.gv), custom_call_target="tpu_custom_call" | custom-call | tf_op jit(solution)/shard_map/hand_out/pallas_call | solution.py:718
